TPU v7x, 256 devices: a whole 4x4x8 slice. The times are simulated.
256 devices in a mesh: query: 32 (over x, z_hi, y), entity: 8 (over z_lo, core).
Axes of the slice: x: 4, y: 4, z: 8 (z_hi: 2, z_lo: 4; z = z_hi * 4 + z_lo), core: 2. Of those that a mesh axis runs over, the one named last changes fastest.
Arguments:
- anchor_ids: int32 [16384], P('query'), may hold values from 0 to 32767
- relation_ids: int32 [16384], P('query'), may hold values from 0 to 4130
- side_flags: int32 [16384], P('query'), may hold values from 0 to 1
- teacher_entities: bfloat16 [32768, 1000], P(('entity', 'query')), may hold values from -1.2 to 1.2, as said below
- student_entities: bfloat16 [32768, 128], P(('entity', 'query')), may hold values from -2.1 to 2.1, as said below
- teacher_relations: bfloat16 [4131, 1000], replicated, may hold values from -9 to 33, as said below
- student_relations: bfloat16 [4131, 128], replicated, may hold values from -9 to 63.6875, as said below
Outputs:
- divergence: float32 [16384], P('query')
- entity_grad: float32 [32768, 128], P(('entity', 'query'))
- query_grad: float32 [16384, 128], P('query')
Inputs may be any that keep to these rules, and one draw needn't show every extreme that they name: `teacher_entities`: Real-valued embeddings. `student_entities`: Real-valued embeddings. `teacher_relations`: Real-valued embeddings. `student_relations`: Real-valued embeddings.
All inputs are finite; a program needn't handle non-finite values.
Results may differ from a plain program's by a relative error of at most 0.013.
Values may be sent and summed in bfloat16 or wider, within the bound.
A program may use at most 128 MiB of HBM per device.

v0:
```python
import jax
import jax.numpy as jnp
from jax import lax
from jax.sharding import PartitionSpec as P


def query_vectors(anchor, relation, flags):
    half = anchor.shape[1] // 2
    sign = (2 * flags - 1).astype(jnp.float32)[:, None]
    a_re = anchor[:, :half]
    a_im = anchor[:, half:]
    r_re = relation[:, :half]
    r_im = relation[:, half:]
    real = a_re * r_re - sign * a_im * r_im
    imag = a_im * r_re + sign * a_re * r_im
    return jnp.concatenate([real, imag], axis=1).astype(jnp.bfloat16)


def per_device(
    anchor_ids,
    relation_ids,
    side_flags,
    teacher_entities,
    student_entities,
    teacher_relations,
    student_relations,
):
    teacher_slab, student_slab = (
        lax.all_gather(teacher_entities, "query", axis=0, tiled=True),
        lax.all_gather(student_entities, "query", axis=0, tiled=True),
    )
    slab = teacher_slab.shape[0]
    offset = lax.axis_index("entity") * slab
    local = anchor_ids - offset
    inside = ((local >= 0) & (local < slab))[:, None]
    safe = jnp.clip(local, 0, slab - 1)
    teacher_part = jnp.where(inside, jnp.take(teacher_slab, safe, axis=0).astype(jnp.float32), 0.0)
    student_part = jnp.where(inside, jnp.take(student_slab, safe, axis=0).astype(jnp.float32), 0.0)
    teacher_anchor, student_anchor = (
        lax.psum(teacher_part.astype(jnp.bfloat16), "entity").astype(jnp.float32),
        lax.psum(student_part.astype(jnp.bfloat16), "entity").astype(jnp.float32),
    )
    query_teacher = query_vectors(
        teacher_anchor,
        jnp.take(teacher_relations, relation_ids, axis=0).astype(jnp.float32),
        side_flags,
    )
    query_student = query_vectors(
        student_anchor,
        jnp.take(student_relations, relation_ids, axis=0).astype(jnp.float32),
        side_flags,
    )
    rows = query_teacher.shape[0]
    block = 1024
    count = slab // block
    teacher_blocks = teacher_slab.reshape(count, block, teacher_slab.shape[1])
    student_blocks = student_slab.reshape(count, block, student_slab.shape[1])

    def first_pass(carry, items):
        top_t, total_t, weighted, top_s, total_s = carry
        t = jnp.dot(query_teacher, items[0].T, preferred_element_type=jnp.float32)
        s = jnp.dot(query_student, items[1].T, preferred_element_type=jnp.float32)
        new_t = jnp.maximum(top_t, jnp.max(t, axis=1))
        factor_t = jnp.exp(top_t - new_t)
        expo_t = jnp.exp(t - new_t[:, None])
        total_t = total_t * factor_t + jnp.sum(expo_t, axis=1)
        weighted = weighted * factor_t + jnp.sum(expo_t * (t - s), axis=1)
        new_s = jnp.maximum(top_s, jnp.max(s, axis=1))
        total_s = total_s * jnp.exp(top_s - new_s) + jnp.sum(jnp.exp(s - new_s[:, None]), axis=1)
        kept = None
        return ((new_t, total_t, weighted, new_s, total_s), kept)

    lowest = jnp.full((rows,), -jnp.inf, jnp.float32)
    nothing = jnp.zeros((rows,), jnp.float32)
    stats, kept = lax.scan(
        first_pass, (lowest, nothing, nothing, lowest, nothing), (teacher_blocks, student_blocks)
    )
    top_t, total_t, weighted, top_s, total_s = stats
    best_t, best_s = lax.pmax((top_t, top_s), "entity")
    factor_t = jnp.exp(top_t - best_t)
    factor_s = jnp.exp(top_s - best_s)
    total_t, weighted, total_s = lax.psum(
        (total_t * factor_t, weighted * factor_t, total_s * factor_s), "entity"
    )
    top_t, top_s = (best_t, best_s)
    divergence = weighted / total_t - top_t - jnp.log(total_t) + top_s + jnp.log(total_s)

    def second_pass(q_grad, items):
        t = jnp.dot(query_teacher, items[0].T, preferred_element_type=jnp.float32)
        s = jnp.dot(query_student, items[1].T, preferred_element_type=jnp.float32)
        prob_t = jnp.exp(t - top_t[:, None]) / total_t[:, None]
        prob_s = jnp.exp(s - top_s[:, None]) / total_s[:, None]
        weights = (prob_s - prob_t).astype(jnp.bfloat16)
        grad_block = jnp.dot(weights.T, query_student, preferred_element_type=jnp.float32)
        q_grad = q_grad + jnp.dot(weights, items[1], preferred_element_type=jnp.float32)
        return (q_grad, grad_block)

    start = jnp.zeros((rows, query_student.shape[1]), jnp.float32)
    q_grad, grad_blocks = lax.scan(second_pass, start, (teacher_blocks, student_blocks))
    slab_grad = grad_blocks.reshape(slab, query_student.shape[1])
    entity_grad = lax.psum_scatter(slab_grad, "query", scatter_dimension=0, tiled=True)
    query_grad = lax.psum(q_grad, "entity")
    return (divergence, entity_grad, query_grad)


def solution(mesh):
    in_specs = (
        P("query"),
        P("query"),
        P("query"),
        P(("entity", "query"), None),
        P(("entity", "query"), None),
        P(),
        P(),
    )
    out_specs = (P("query"), P(("entity", "query"), None), P("query", None))
    return jax.shard_map(
        per_device, mesh=mesh, in_specs=in_specs, out_specs=out_specs, check_vma=False
    )
```

profile of v0, /device:TPU:32, one launch (start us, length us, event | category | flops | bytes accessed | tf_op | source)
XLA Modules:
  0.0 744.2 jit_solution(13715478936245018552)
XLA Ops:
  8.0 1.8 copy.10
  10.6 83.7 %all-gather.5.cloned.1.call-done = bf16[4096,128]{1,0:T(8,128)(2,1)} async-done(((bf16[128,128]{1,0:T(8,128)(2,1)}), bf16[4096,128]{1,0:T(8,128)(2,1)}) %all-gather.5.cloned.1.call-update) | async-done | bytes 1048592 | tf_op jit(solution)/shard_map/all_gather | solution.py:30
  94.3 2.4 gather_fusion.2
  96.7 0.9 select_convert_fusion.2
  97.5 149.9 %all-gather.3.cloned.1.call-done = bf16[4096,1000]{1,0:T(8,128)(2,1)} async-done(((bf16[128,1000]{1,0:T(8,128)(2,1)}), bf16[4096,1000]{1,0:T(8,128)(2,1)}) %all-gather.3.cloned.1.call-update) | async-done | bytes 8192016 | tf_op jit(solution)/shard_map/all_gather | solution.py:29
  247.4 7.2 gather_fusion
  254.6 1.3 select_convert_fusion
  256.1 12.1 %copy.11 = bf16[4131,1000]{1,0:T(8,128)(2,1)} copy(bf16[4131,1000]{0,1:T(8,128)(2,1)} %param.16) | data formatting | bytes 16524000 | tf_op args[5]
  268.3 8.0 %gather_fusion.1 = bf16[512,1000]{1,0:T(8,128)(2,1)} fusion(bf16[4131,1000]{1,0:T(8,128)(2,1)} %copy.11, s32[1024]{0:T(1024)S(1)} %pad_clamp_fusion), kind=kCustom, calls=%fused_computation.1 | custom fusion | bytes 2050048 | tf_op jit(solution)/shard_map/jit(_take)/gather | solution.py:45
  276.3 1.3 gather_fusion.3
  278.3 0.8 select_convert_fusion.3
  279.1 1.4 select_convert_fusion.1
  280.6 43.3 %all-reduce.8.cloned.1.call-done = (bf16[512,1000]{1,0:T(8,128)(2,1)}, bf16[512,128]{1,0:T(8,128)(2,1)}) async-done(((bf16[512,1000]{1,0:T(8,128)(2,1)}, bf16[512,128]{1,0:T(8,128)(2,1)}), (bf16[512,1000]{1,0:T(8,128)(2,1)}, bf16[512,128]{1,0:T(8,128)(2,1)})) %all-reduce.8.cloned.1.call-update) | async-done | bytes 1155088 | tf_op jit(solution)/shard_map/psum | solution.py:40
  323.9 1.5 convert_element_type.33
  325.4 1.0 subtract_convert_fusion.1
  326.4 1.3 pad_maximum_fusion
  328.1 46.0 %while.32 = (s32[]{:T(128)}, f32[512]{0:T(512)S(1)}, f32[512]{0:T(512)}, f32[512]{0:T(512)}, f32[512]{0:T(512)}, /*index=5*/f32[512]{0:T(512)}, bf16[4,1024,1000...) while((s32[]{:T(128)}, f32[512]{0:T(512)S(1)}, ...), condition=%wide.region_8.9_spmd.clone, body=%wide.region_2.8_spmd.clone.sunk | while | flops 1187518464 | bytes 12046677 | solution.py:75
  328.1 5.1 fusion.51
  333.2 2.0 fusion.52
  336.6 2.4 multiply_reduce_fusion.2
  339.6 5.1 fusion.51
  344.7 2.0 fusion.52
  348.1 2.4 multiply_reduce_fusion.2
  351.2 5.1 fusion.51
  356.2 2.0 fusion.52
  359.6 2.4 multiply_reduce_fusion.2
  362.7 5.1 fusion.51
  367.7 2.0 fusion.52
  371.1 2.4 multiply_reduce_fusion.2
  374.2 14.8 %all-reduce.1 = (f32[512]{0:T(512)}, f32[512]{0:T(512)}) all-reduce(f32[512]{0:T(512)} %get-tuple-element.120, f32[512]{0:T(512)S(1)} %get-tuple-element.118), channel_id=1, replica_groups=mesh['query'=32,'entity'=8] {'entity'}, use_global_device_ids=true, to_apply=%region_12.13 | all-reduce | flops 1024 | bytes 8192 | tf_op jit(solution)/shard_map/pmax | solution.py:79
  389.7 14.6 %all-reduce = (f32[512]{0:T(512)S(1)}, f32[512]{0:T(512)}, f32[512]{0:T(512)}) all-reduce(f32[512]{0:T(512)S(1)} %get-tuple-element.261, f32[512]{0:T(512)S(1)} %get-tuple-element.259, f32[512]{0:T(512)S(1)} %get-tuple-element.258), channel_id=1, replica_groups=mesh['query'=32,'entity'=8] {'entity'}, use_global_device_ids=true, to_apply=%region_13.14 | all-reduce | flops 1536 | bytes 12288 | tf_op jit(solution)/shard_map/psum | solution.py:82
  404.3 26.0 %while.33 = (s32[]{:T(128)}, f32[512,128]{1,0:T(8,128)S(1)}, f32[4,1024,128]{2,1,0:T(8,128)}, bf16[4,1024,128]{2,1,0:T(8,128)(2,1)}, bf16[512,128]{1,0:T(8,128)(...) while((s32[]{:T(128)}, f32[512,128]{1,0:T(8,128)S(1)}, ...), condition=%wide.region_15.16_spmd.clone, body=%wide.region_14.15_spmd.clone.sunk | while | flops 1454505984 | bytes 16531671 | solution.py:99
  404.3 3.2 fusion.62
  407.6 1.5 subtract_convert_fusion.4
  409.6 1.2 fusion.63
  410.8 3.2 fusion.62
  414.1 1.5 subtract_convert_fusion.4
  416.1 1.2 fusion.63
  417.3 3.2 fusion.62
  420.6 1.5 subtract_convert_fusion.4
  422.6 1.2 fusion.63
  423.8 3.2 fusion.62
  427.1 1.5 subtract_convert_fusion.4
  429.1 1.2 fusion.63
  431.6 1.3 log_add_fusion
  432.9 69.5 %all-reduce.6.cloned.1.call-done = f32[512,128]{1,0:T(8,128)} async-done(((f32[512,128]{1,0:T(8,128)}), f32[512,128]{1,0:T(8,128)}) %all-reduce.6.cloned.1.call-update) | async-done | bytes 262160 | tf_op jit(solution)/shard_map/psum | solution.py:102
  502.4 233.6 %reduce-scatter.2.cloned.1.call-done = f32[128,128]{1,0:T(8,128)} async-done(((f32[4096,128]{1,0:T(8,128)}), f32[128,128]{1,0:T(8,128)}) %reduce-scatter.2.cloned.1.call-update) | async-done | bytes 65552 | tf_op jit(solution)/shard_map/reduce_scatter | solution.py:101
  736.0 1.7 copy.43
  (141 shorter events, 14.7 us)
Async XLA Ops:
  7.2 269.1 %copy-start = (bf16[4131,128]{1,0:T(8,128)(2,1)S(1)}, bf16[4131,128]{1,0:T(8,128)(2,1)}, u32[]{:S(2)}) copy-start(bf16[4131,128]{1,0:T(8,128)(2,1)} %param.17) | copy-start | bytes 3172612
  7.2 87.1 %all-gather.5.cloned.1.call-start = ((), (), s32[]{:S(2)}) async-start(), calls=%async_computation.2 | async-start | bytes 1081344 | tf_op jit(solution)/shard_map/all_gather | solution.py:30
  7.9 239.5 %all-gather.3.cloned.1.call-start = ((), (), s32[]{:S(2)}) async-start(), calls=%async_computation.1 | async-start | bytes 8650752 | tf_op jit(solution)/shard_map/all_gather | solution.py:29
  9.8 314.0 %all-reduce.8.cloned.1.call-start = ((), (), s32[]{:S(2)}) async-start(), calls=%async_computation.5 | async-start | bytes 2359296 | tf_op jit(solution)/shard_map/psum | solution.py:40
  254.6 1.4 copy-start.13
  256.0 246.4 %all-reduce.6.cloned.1.call-start = ((), (), s32[]{:S(2)}) async-start(), calls=%async_computation.4 | async-start | bytes 524288 | tf_op jit(solution)/shard_map/psum | solution.py:102
  268.3 9.4 %copy-start.14 = (s32[512]{0:T(512)S(1)}, s32[512]{0:T(512)}, u32[]{:S(2)}) copy-start(s32[512]{0:T(512)} %param.13) | copy-start | bytes 6148
  323.9 1.5 copy-start.5
  323.9 1.5 copy-start.12
  326.4 1.3 copy-start.3
  336.5 2.4 copy-start.4
  336.5 2.4 copy-start.6
  336.5 2.4 copy-start.8
  336.6 2.4 copy-start.10
  339.0 0.6 copy-start.7
  339.0 0.6 copy-start.9
  339.0 0.6 copy-start.11
  348.1 2.4 copy-start.4
  348.1 2.4 copy-start.6
  348.1 2.4 copy-start.8
  348.1 2.4 copy-start.10
  350.5 0.6 copy-start.7
  350.5 0.6 copy-start.9
  350.5 0.6 copy-start.11
  359.6 2.4 copy-start.4
  359.6 2.4 copy-start.6
  359.6 2.4 copy-start.8
  359.6 2.4 copy-start.10
  362.0 0.6 copy-start.7
  362.0 0.6 copy-start.9
  371.1 2.4 copy-start.4
  371.1 2.4 copy-start.6
  371.1 2.4 copy-start.8
  371.1 2.4 copy-start.10
  373.5 0.6 copy-start.7
  373.5 0.6 copy-start.9
  404.3 3.2 copy-start.1
  404.3 3.2 copy-start.15
  410.8 3.2 copy-start.1
  410.8 3.2 copy-start.15
  417.3 3.2 copy-start.1
  417.3 3.2 copy-start.15
  423.8 3.2 copy-start.1
  423.8 3.2 copy-start.15
  430.3 0.7 copy-start.2
  430.3 1.3 copy-start.16
  430.3 1.3 copy-start.17
  431.0 305.0 %reduce-scatter.2.cloned.1.call-start = ((), (), s32[]{:S(2)}) async-start(), calls=%async_computation.3 | async-start | bytes 2162688 | tf_op jit(solution)/shard_map/reduce_scatter | solution.py:101
  (2 other events, 1.2 us)
Sparse Core Ops, SparseCore 0:
  11.4 82.7 all-gather.4
  98.4 149.0 all-gather.2
  256.1 67.6 all-reduce.7
  431.1 71.2 all-reduce.5
  505.5 230.4 reduce-scatter.1
where the time goes:
time: 745 us; the launch traced here: 744 us
  waiting for transfers between devices  581 us (78%)
  matrix products  53.9 us (7%)
  local copies, waits for them, and re-layouts  37.8 us (5%)
  blocking collectives  29.4 us (4%)
  other arithmetic  27 us (4%)
  between operations  14 us (2%)
    reduce_scatter x1, waiting for transfers between devices, per_device(): lax.psum_scatter(slab_grad, 'query', scatter_dimension=0, tiled=True)  234 us
    all_gather x1, waiting for transfers between devices, per_device(): lax.all_gather(teacher_entities, 'query', axis=0, tiled=True)  150 us
    all_gather x1, waiting for transfers between devices, per_device(): lax.all_gather(student_entities, 'query', axis=0, tiled=True)  83.7 us
    psum x1, waiting for transfers between devices, per_device(): query_grad = lax.psum(q_grad, 'entity')  69.5 us
    psum x1, waiting for transfers between devices, per_device(): lax.psum(teacher_part.astype(jnp.bfloat16), 'entity').astype(jnp.float32)  43.3 us
    dot_general x4, matrix products, first_pass(): t = jnp.dot(query_teacher, items[0].T, preferred_element_type=jnp.float32)  20.3 us
    unnamed x21, local copies, waits for them, and re-layouts  16.4 us
  transfers between devices with their start and end apart: 5, of which 5 were waited for; matrix products, arithmetic and copies ran while one was open for 4% of the time, Pallas kernels for 0%

commit v1 on v0

v1 whole, which is shorter than its diff:
```python
import jax
import jax.numpy as jnp
from jax import lax
from jax.experimental import pallas as pl
from jax.experimental.pallas import tpu as pltpu
from jax.sharding import PartitionSpec as P

MESH = pl.DeviceIdType.MESH
BF = jnp.bfloat16
F32 = jnp.float32
GROUP = 512
ROWS = 2 * GROUP
ENT = 128
HALF = 500
PAD = 512
BLK = ENT + 2 * PAD
CUT = BLK // 2
REL = 4131
RELA = 4096
SHARD = 64
BIT = 32


def slot(sd, fd):
    return sd * 4 + fd


def dot_nn(a, b):
    return lax.dot_general(a, b, (((1,), (0,)), ((), ())), preferred_element_type=F32)


def dot_nt(a, b):
    return lax.dot_general(a, b, (((1,), (1,)), ((), ())), preferred_element_type=F32)


def kernel(
    meta,
    ent_t,
    ent_s,
    rel_t,
    rel_s,
    div_out,
    eg_out,
    qg_out,
    slab,
    rtv,
    rsv,
    wide,
    mids,
    mrow,
    mcol,
    idb,
    abuf,
    dbuf,
    sumb,
    rbuf,
    racc,
    rsacc,
    qbuf,
    tbuf,
    sbuf,
    mxt,
    mxs,
    zt_acc,
    w_acc,
    zs_acc,
    own_st,
    mate_st,
    st,
    fin,
    ftb,
    fsb,
    qst,
    eg_own,
    eg_s,
    eg_sr,
    eg_f,
    eg_fr,
    qg,
    qgb,
    qgd,
    qgsum,
    qgz,
    qgr,
    qgo,
    loc_sem,
    send_sem,
    recv_sem,
):
    q = lax.axis_index("query")
    e = lax.axis_index("entity")
    x, zh, y = lax.div(q, 8), lax.rem(lax.div(q, 4), 2), lax.rem(q, 4)
    zl, core = lax.div(e, 2), lax.rem(e, 2)
    z = zh * 4 + zl
    first = x + core * (y - x)
    second = y + core * (x - y)

    def dev(fd, sd):
        a, b = lax.rem(first + fd, 4), lax.rem(second + sd, 4)
        return (a + core * (b - a)) * 8 + zh * 4 + b + core * (a - b)

    def zdev(d):
        zz = lax.rem(z + d, 8)
        return (x * 8 + lax.div(zz, 4) * 4 + y, lax.rem(zz, 4) * 2 + core)

    mate = (q, zl * 2 + 1 - core)

    rt_copy = pltpu.make_async_copy(rel_t, rtv, loc_sem.at[0])
    rt_copy.start()
    rs_copy = pltpu.make_async_copy(rel_s, rsv, loc_sem.at[1])
    rs_copy.start()

    barrier = pltpu.get_barrier_semaphore()
    peers = [(dev(d, 0), e) for d in (1, 2, 3)]
    peers += [(dev(0, d), e) for d in (1, 2, 3)]
    peers += [zdev(d) for d in range(1, 8)]
    peers += [mate]
    for peer in peers:
        pl.semaphore_signal(barrier, inc=1, device_id=peer, device_id_type=MESH)

    slab[0, 0:ENT, :] = ent_s[...]
    wide[0 : 2 * HALF, :] = ent_t[...].astype(F32)
    wide[2 * HALF : 2 * PAD, :] = jnp.zeros((2 * PAD - 2 * HALF, ENT), F32)
    row = lax.broadcasted_iota(jnp.int32, (PAD, ENT), 0)
    slab[0, ENT : ENT + PAD, :] = jnp.where(row < HALF, wide[0:PAD, :], 0.0).astype(BF)
    slab[0, ENT + PAD : BLK, :] = pltpu.roll(wide[...], 2 * PAD - HALF, 0)[0:PAD].astype(BF)
    mids[zh] = jnp.zeros((8, GROUP), jnp.int32)
    mids[zh, 0:3, :] = meta[...]
    pl.semaphore_wait(barrier, len(peers))

    sent = []
    numbers = {}

    def ship(key, src, dst, target):
        n = len(sent)
        numbers[key] = n
        copy = pltpu.make_async_remote_copy(
            src_ref=src,
            dst_ref=dst,
            send_sem=send_sem.at[n],
            recv_sem=recv_sem.at[n],
            device_id=target,
            device_id_type=MESH,
        )
        copy.start()
        sent.append(copy)

    def await_at(key, dst):
        n = numbers[key]
        pltpu.make_async_remote_copy(
            src_ref=dst,
            dst_ref=dst,
            send_sem=send_sem.at[n],
            recv_sem=recv_sem.at[n],
            device_id=mate,
            device_id_type=MESH,
        ).wait_recv()

    def block(k, half=None):
        if half is None:
            return slab.at[k]
        return slab.at[k, pl.ds(half * CUT, CUT), :]

    def push(src, dst, target, half=None):
        ship(("slab", dst, half), block(src, half), block(dst, half), (target, e))

    def got(k, half=None):
        await_at(("slab", k, half), block(k, half))

    def f_start():
        push(slot(0, 0), slot(0, 3), dev(1, 0))
        push(slot(0, 0), slot(0, 1), dev(3, 0))

    def s_start(fd):
        push(slot(0, fd), slot(3, fd), dev(0, 1))
        push(slot(0, fd), slot(1, fd), dev(0, 3))

    def f_step(fd):
        got(slot(0, fd))
        push(slot(0, fd), slot(0, 2), dev(1 if fd == 3 else 3, 0), 0 if fd == 3 else 1)
        s_start(fd)

    def f_last():
        got(slot(0, 2), 0)
        got(slot(0, 2), 1)
        s_start(2)

    def s_step(fd):
        got(slot(3, fd))
        push(slot(3, fd), slot(2, fd), dev(0, 1), 0)
        got(slot(1, fd))
        push(slot(1, fd), slot(2, fd), dev(0, 3), 1)

    lane = lax.broadcasted_iota(jnp.int32, (ROWS, ENT), 1)

    def one_hot(ids, at):
        return jnp.where(ids - at == lane[: ids.shape[0]], 1.0, 0.0).astype(BF)

    def pick(sd, new=False):
        ks = [slot(sd, fd) for fd in range(4)]
        hot = jnp.concatenate(
            [one_hot(idb[...], e * 4096 + dev(fd, sd) * ENT) for fd in range(4)], axis=1
        )
        value = dot_nn(hot, jnp.concatenate([slab[k, 0:ENT, :] for k in ks], axis=0))
        tbuf[4, :, 0:ENT] = value if new else tbuf[4, :, 0:ENT] + value
        for h in range(4):
            lo = ENT + h * 256
            right = jnp.concatenate([slab[k, lo : lo + 256, :] for k in ks], axis=1)
            value = dot_nt(hot, right)
            tbuf[h] = value if new else tbuf[h] + value

    mine = pl.multiple_of(core * GROUP + z * SHARD, SHARD)

    def relations():
        ids = jnp.broadcast_to(mcol[pl.ds(mine, SHARD), 1:2], (SHARD, ENT)).astype(jnp.int32)
        left = REL - RELA
        hot = one_hot(ids, RELA)[:, 0:left]
        racc[...] = jnp.zeros_like(racc)
        racc[:, 0 : 2 * HALF] = dot_nt(hot, rtv[:, RELA:REL])
        rsacc[...] = dot_nn(hot, rsv[RELA:REL, :])

        @pl.loop(0, RELA // 512)
        def _(c):
            at = pl.multiple_of(c * 512, 512)
            hots = jnp.concatenate([one_hot(ids, at + j * ENT) for j in range(4)], axis=1)
            racc[:, 0 : 2 * HALF] += dot_nt(hots, rtv[:, pl.ds(at, 512)])
            rsacc[...] += dot_nn(hots, rsv[pl.ds(at, 512), :])

    f_start()
    s_start(0)
    ship("ids", mids.at[zh], mids.at[zh], zdev(4))
    f_step(3)
    f_step(1)
    await_at("ids", mids.at[1 - zh])
    mrow[...] = jnp.zeros_like(mrow)
    for g in range(2):
        mrow[0:8, :] = mids[g].astype(F32)
        flat = jnp.transpose(mrow[...])
        mcol[g * GROUP : (g + 1) * GROUP, :] = flat
        wanted = jnp.broadcast_to(flat[:, 0:1], (GROUP, ENT)).astype(jnp.int32)
        idb[g * GROUP : (g + 1) * GROUP, :] = wanted
    f_last()
    s_step(0)
    rt_copy.wait()
    rs_copy.wait()
    relations()
    s_step(3)
    s_step(1)
    pick(0, True)
    s_step(2)
    pick(3)
    pick(1)
    for fd in range(4):
        got(slot(2, fd), 0)
        got(slot(2, fd), 1)
    pick(2)

    abuf[:, 0:ENT] = tbuf[4, :, 0:ENT].astype(BF)
    for h in range(4):
        abuf[:, ENT + h * 256 : ENT + (h + 1) * 256] = tbuf[h].astype(BF)
    other = pl.multiple_of((1 - core) * GROUP, GROUP)
    ship("pair", abuf.at[pl.ds(other, GROUP), :], dbuf, mate)
    await_at("pair", dbuf)
    kept = pl.multiple_of(core * GROUP, GROUP)
    sumb[...] = (abuf[pl.ds(kept, GROUP), :].astype(F32) + dbuf[...].astype(F32)).astype(BF)

    def part(d, half):
        return pl.ds(pl.multiple_of(lax.rem(z + d, 8) * SHARD + half * BIT, BIT), BIT)

    def chain(way, role):
        return role if way == 0 else 1 - role

    def ring_send(way, role, j):
        d = j if way == 0 else 8 - j
        rows = part(d, chain(way, role))
        at = way * 7 + role * 4 + (4 - role) - j
        ship(("ring", way, role, j), sumb.at[rows, :], rbuf.at[at], zdev(1 if way == 0 else 7))

    def ring_wait(way, role, j):
        at = way * 7 + role * 4 + (4 - role) - j
        await_at(("ring", way, role, j), rbuf.at[at])
        return rbuf[at].astype(F32)

    for way in range(2):
        ring_send(way, 0, 4)
    for way in range(2):
        ring_send(way, 1, 3)
    for role, j in ((0, 4), (1, 3), (0, 3), (1, 2), (0, 2)):
        for way in range(2):
            came = ring_wait(way, role, j)
            d = j - 1 if way == 0 else 9 - j
            rows = part(d, chain(way, role))
            sumb[rows, :] = (sumb[rows, :].astype(F32) + came).astype(BF)
            ring_send(way, role, j - 1)
    halves = [sumb[part(0, h), :].astype(F32) for h in range(2)]
    for role in (1, 0):
        for way in range(2):
            h = chain(way, role)
            halves[h] = halves[h] + ring_wait(way, role, 1)
    anchor = jnp.concatenate(halves, axis=0)

    sign = 2.0 * mcol[pl.ds(mine, SHARD), 2:3] - 1.0
    a_s, r_s = anchor[:, 0:ENT], rsacc[...]
    a_w, r_w = pltpu.roll(a_s, 64, 1), pltpu.roll(r_s, 64, 1)
    low = lane[:SHARD] < 64
    q_s = jnp.where(low, a_s * r_s - sign * a_w * r_w, a_s * r_w + sign * a_w * r_s)
    a_re, a_im = anchor[:, ENT : ENT + PAD], anchor[:, ENT + PAD : BLK]
    whole = racc[...]
    r_re, r_im = whole[:, 0:PAD], pltpu.roll(whole, 2 * PAD - HALF, 1)[:, 0:PAD]
    qbuf[pl.ds(mine, SHARD), 0:ENT] = q_s.astype(BF)
    qbuf[pl.ds(mine, SHARD), ENT : ENT + PAD] = (a_re * r_re - sign * a_im * r_im).astype(BF)
    qbuf[pl.ds(mine, SHARD), ENT + PAD : BLK] = (a_im * r_re + sign * a_re * r_im).astype(BF)

    def bit(d, half, other=False):
        c = 1 - core if other else core
        at = c * GROUP + lax.rem(z + d, 8) * SHARD + half * BIT
        return qbuf.at[pl.ds(pl.multiple_of(at, BIT), BIT), :]

    def ring_pass(way, role, j):
        d = 8 - (j - 1) if way == 0 else j - 1
        here = bit(d, chain(way, role))
        ship(("pass", way, role, j), here, here, zdev(1 if way == 0 else 7))

    for role in range(2):
        for way in range(2):
            ring_pass(way, role, 1)
    for h in range(2):
        ship(("mate", 0, h), bit(0, h), bit(0, h), mate)
    came = [(0, h) for h in range(2)]
    for role, j in ((0, 1), (1, 1), (0, 2), (1, 2), (0, 3), (1, 3), (0, 4)):
        for way in range(2):
            h = chain(way, role)
            d = 8 - j if way == 0 else j
            await_at(("pass", way, role, j), bit(d, h))
            if j < 4 - role:
                ring_pass(way, role, j + 1)
            ship(("mate", d, h), bit(d, h), bit(d, h), mate)
            came.append((d, h))
    for d, h in came:
        await_at(("mate", d, h), bit(d, h, True))

    mxt[...] = jnp.full_like(mxt, -jnp.inf)
    mxs[...] = jnp.full_like(mxs, -jnp.inf)

    @pl.loop(0, 8)
    def _(p):
        k = 2 * p
        right = jnp.concatenate([slab[k, ENT:BLK, :], slab[k + 1, ENT:BLK, :]], axis=1)
        t = dot_nn(qbuf[:, ENT:BLK], right)
        right = jnp.concatenate([slab[k, 0:ENT, :], slab[k + 1, 0:ENT, :]], axis=0)
        s = dot_nt(qbuf[:, 0:ENT], right)
        tbuf[p] = t
        sbuf[p] = s
        mxt[...] = jnp.maximum(mxt[...], jnp.maximum(t[:, 0:ENT], t[:, ENT:]))
        mxs[...] = jnp.maximum(mxs[...], jnp.maximum(s[:, 0:ENT], s[:, ENT:]))

    mxt[...] = jnp.broadcast_to(jnp.max(mxt[...], axis=1, keepdims=True), (ROWS, ENT))
    mxs[...] = jnp.broadcast_to(jnp.max(mxs[...], axis=1, keepdims=True), (ROWS, ENT))

    @pl.loop(0, ROWS // 64)
    def _(r):
        rows = pl.ds(pl.multiple_of(r * 64, 64), 64)
        top_t, top_s = mxt[rows, :], mxs[rows, :]

        def step(p, carry):
            zt, w, zs = carry
            for h in range(2):
                cols = slice(h * ENT, (h + 1) * ENT)
                t, s = tbuf[p, rows, cols], sbuf[p, rows, cols]
                et, es = jnp.exp(t - top_t), jnp.exp(s - top_s)
                zt, w, zs = zt + et, w + et * (t - s), zs + es
                tbuf[p, rows, cols] = et
                sbuf[p, rows, cols] = es
            return zt, w, zs

        zero = jnp.zeros((64, ENT), F32)
        zt, w, zs = lax.fori_loop(0, 8, step, (zero, zero, zero))
        zt_acc[rows, :] = zt
        w_acc[rows, :] = w
        zs_acc[rows, :] = zs

    table = jnp.where(lane == 0, mxt[...], 0.0)
    table = jnp.where(lane == 1, jnp.sum(zt_acc[...], axis=1, keepdims=True), table)
    table = jnp.where(lane == 2, jnp.sum(w_acc[...], axis=1, keepdims=True), table)
    table = jnp.where(lane == 3, mxs[...], table)
    table = jnp.where(lane == 4, jnp.sum(zs_acc[...], axis=1, keepdims=True), table)
    flat = jnp.transpose(table)[0:8, :]
    own_st[0] = flat[:, 0:GROUP]
    own_st[1] = flat[:, GROUP:ROWS]
    ship("pair stats", own_st.at[1 - core], mate_st, mate)
    qst[...] = jnp.transpose(qbuf[:, 0:ENT].astype(F32)).astype(BF)
    await_at("pair stats", mate_st)

    def merge(tables):
        top_t, top_s = tables[0][0:1, :], tables[0][3:4, :]
        for v in tables[1:]:
            top_t, top_s = jnp.maximum(top_t, v[0:1, :]), jnp.maximum(top_s, v[3:4, :])
        total_t = weighted = total_s = jnp.zeros((1, GROUP), F32)
        for v in tables:
            scale_t, scale_s = jnp.exp(v[0:1, :] - top_t), jnp.exp(v[3:4, :] - top_s)
            total_t = total_t + v[1:2, :] * scale_t
            weighted = weighted + v[2:3, :] * scale_t
            total_s = total_s + v[4:5, :] * scale_s
        return top_t, total_t, weighted, top_s, total_s

    st[z] = jnp.zeros((8, GROUP), F32)
    for i, v in enumerate(merge([own_st[core], mate_st[...]])):
        st[z, i : i + 1, :] = v
    for d in range(1, 8):
        ship(("stats", d), st.at[z], st.at[z], zdev(d))
    for d in range(1, 8):
        await_at(("stats", d), st.at[lax.rem(z + 8 - d, 8)])
    top_t, total_t, weighted, top_s, total_s = merge([st[i] for i in range(8)])
    divergence = weighted / total_t - top_t - jnp.log(total_t) + top_s + jnp.log(total_s)
    fin[core] = jnp.zeros((8, GROUP), F32)
    for i, v in enumerate((top_t, total_t, divergence, top_s, total_s)):
        fin[core, i : i + 1, :] = v
    ship("final", fin.at[core], fin.at[core], mate)
    await_at("final", fin.at[1 - core])
    div_out[...] = fin[zh, 2:3, :]
    rowi = lax.broadcasted_iota(jnp.int32, (ENT, GROUP), 0)
    for g in range(2):
        f_t = jnp.exp(own_st[g, 0:1, :] - fin[g, 0:1, :]) / fin[g, 1:2, :]
        f_s = jnp.exp(own_st[g, 3:4, :] - fin[g, 3:4, :]) / fin[g, 4:5, :]
        flipped = jnp.transpose(jnp.where(rowi == 0, f_t, jnp.where(rowi == 1, f_s, 0.0)))
        ftb[g * GROUP : (g + 1) * GROUP, :] = jnp.broadcast_to(flipped[:, 0:1], (GROUP, ENT))
        fsb[g * GROUP : (g + 1) * GROUP, :] = jnp.broadcast_to(flipped[:, 1:2], (GROUP, ENT))

    qg[...] = jnp.zeros_like(qg)
    for sd in (2, 1, 3, 0):

        @pl.loop(0, 2)
        def _(i, sd=sd):
            p = sd * 2 + i
            halves = []
            for h in range(2):
                cols = slice(h * ENT, (h + 1) * ENT)
                g = sbuf[p, :, cols] * fsb[...] - tbuf[p, :, cols] * ftb[...]
                halves.append(g.astype(BF))
            g = jnp.concatenate(halves, axis=1)
            grad = dot_nn(qst[...], g)
            for h in range(2):
                cols = slice(h * ENT, (h + 1) * ENT)
                if sd:
                    eg_s[sd - 1, 2 * i + h] = grad[:, cols].astype(BF)
                else:
                    eg_own[2 * i + h] = grad[:, cols]
            right = jnp.concatenate([slab[2 * p, 0:ENT, :], slab[2 * p + 1, 0:ENT, :]], axis=0)
            qg[...] += dot_nn(g, right)

        if sd:
            ship(("second", sd), eg_s.at[sd - 1], eg_sr.at[sd - 1], (dev(0, sd), e))

    qgb[...] = qg[pl.ds(other, GROUP), :].astype(BF)
    ship("pair grad", qgb, qgd, mate)
    for sd in (1, 3, 2):
        await_at(("second", sd), eg_sr.at[sd - 1])
    for fd in (2, 1, 3, 0):
        v = eg_own[fd]
        for sd in (1, 2, 3):
            v = v + eg_sr[sd - 1, fd].astype(F32)
        if fd:
            eg_f[fd - 1] = v.astype(BF)
            ship(("first", fd), eg_f.at[fd - 1], eg_fr.at[fd - 1], (dev(fd, 0), e))
        else:
            near = v
    await_at("pair grad", qgd)
    qgsum[...] = qg[pl.ds(kept, GROUP), :] + qgd[...].astype(F32)
    qgz[...] = qgsum[...].astype(BF)
    for d in range(1, 8):
        at = pl.multiple_of(lax.rem(z + d, 8) * SHARD, SHARD)
        ship(("shard", d), qgz.at[pl.ds(at, SHARD), :], qgr.at[d - 1], zdev(d))
    for fd in (1, 3, 2):
        await_at(("first", fd), eg_fr.at[fd - 1])
    for fd in (1, 2, 3):
        near = near + eg_fr[fd - 1].astype(F32)
    eg_out[...] = jnp.transpose(near)
    total = qgsum[pl.ds(pl.multiple_of(z * SHARD, SHARD), SHARD), :]
    for d in range(1, 8):
        await_at(("shard", d), qgr.at[d - 1])
    for d in range(1, 8):
        total = total + qgr[d - 1].astype(F32)

    def out_rows(d):
        return qgo.at[core, pl.ds(pl.multiple_of(lax.rem(z + d, 8) * SHARD, SHARD), SHARD), :]

    qgo[core, pl.ds(pl.multiple_of(z * SHARD, SHARD), SHARD), :] = total.astype(BF)
    for d in range(1, 8):
        ship(("sum", d), out_rows(0), out_rows(0), zdev(d))
    for d in range(1, 8):
        await_at(("sum", d), out_rows(8 - d))
    ship("pair sum", qgo.at[core], qgo.at[core], mate)
    await_at("pair sum", qgo.at[1 - core])
    qg_out[...] = qgo[zh].astype(F32)

    for copy in sent:
        copy.wait_send()


def per_device(
    anchor_ids,
    relation_ids,
    side_flags,
    teacher_entities,
    student_entities,
    teacher_relations,
    student_relations,
):
    meta = jnp.stack([anchor_ids, relation_ids, side_flags], axis=0)
    vmem = pl.BlockSpec(memory_space=pltpu.VMEM)
    hbm = pl.BlockSpec(memory_space=pl.ANY)
    big = (ROWS, ENT)
    div, eg, qg = pl.pallas_call(
        kernel,
        out_shape=(
            jax.ShapeDtypeStruct((1, GROUP), F32),
            jax.ShapeDtypeStruct((ENT, ENT), F32),
            jax.ShapeDtypeStruct((GROUP, ENT), F32),
        ),
        in_specs=[vmem, vmem, vmem, hbm, hbm],
        out_specs=(vmem, vmem, vmem),
        scratch_shapes=[
            pltpu.VMEM((16, BLK, ENT), BF),
            pltpu.VMEM((2 * HALF, REL), BF),
            pltpu.VMEM((REL, ENT), BF),
            pltpu.VMEM((2 * PAD, ENT), F32),
            pltpu.VMEM((2, 8, GROUP), jnp.int32),
            pltpu.VMEM((ENT, GROUP), F32),
            pltpu.VMEM(big, F32),
            pltpu.VMEM(big, jnp.int32),
            pltpu.VMEM((ROWS, BLK), BF),
            pltpu.VMEM((GROUP, BLK), BF),
            pltpu.VMEM((GROUP, BLK), BF),
            pltpu.VMEM((14, BIT, BLK), BF),
            pltpu.VMEM((SHARD, 2 * PAD), F32),
            pltpu.VMEM((SHARD, ENT), F32),
            pltpu.VMEM((ROWS, BLK), BF),
            pltpu.VMEM((8, ROWS, 256), F32),
            pltpu.VMEM((8, ROWS, 256), F32),
            pltpu.VMEM(big, F32),
            pltpu.VMEM(big, F32),
            pltpu.VMEM(big, F32),
            pltpu.VMEM(big, F32),
            pltpu.VMEM(big, F32),
            pltpu.VMEM((2, 8, GROUP), F32),
            pltpu.VMEM((8, GROUP), F32),
            pltpu.VMEM((8, 8, GROUP), F32),
            pltpu.VMEM((2, 8, GROUP), F32),
            pltpu.VMEM(big, F32),
            pltpu.VMEM(big, F32),
            pltpu.VMEM((ENT, ROWS), BF),
            pltpu.VMEM((4, ENT, ENT), F32),
            pltpu.VMEM((3, 4, ENT, ENT), BF),
            pltpu.VMEM((3, 4, ENT, ENT), BF),
            pltpu.VMEM((3, ENT, ENT), BF),
            pltpu.VMEM((3, ENT, ENT), BF),
            pltpu.VMEM(big, F32),
            pltpu.VMEM((GROUP, ENT), BF),
            pltpu.VMEM((GROUP, ENT), BF),
            pltpu.VMEM((GROUP, ENT), F32),
            pltpu.VMEM((GROUP, ENT), BF),
            pltpu.VMEM((7, SHARD, ENT), BF),
            pltpu.VMEM((2, GROUP, ENT), BF),
            pltpu.SemaphoreType.DMA((2,)),
            pltpu.SemaphoreType.DMA((110,)),
            pltpu.SemaphoreType.DMA((110,)),
        ],
        compiler_params=pltpu.CompilerParams(
            collective_id=0, has_side_effects=True, vmem_limit_bytes=60 * 2**20
        ),
    )(meta, teacher_entities.T, student_entities, teacher_relations.T, student_relations)
    return div.reshape(GROUP), eg, qg


def solution(mesh):
    in_specs = (
        P("query"),
        P("query"),
        P("query"),
        P(("entity", "query"), None),
        P(("entity", "query"), None),
        P(),
        P(),
    )
    out_specs = (P("query"), P(("entity", "query"), None), P("query", None))
    return jax.shard_map(
        per_device, mesh=mesh, in_specs=in_specs, out_specs=out_specs, check_vma=False
    )
```

time: 745 us -> 125 us (0.17)
  the two profiles are of different devices: /device:TPU:32 before, /device:TPU:1 now
where the time goes in v1:
time: 125 us
  Pallas kernels  119 us (95%)
  local copies, waits for them, and re-layouts  4.4 us (4%)
  other arithmetic  1.32 us (1%)
    pallas_call x1, Pallas kernels, per_device(): pl.pallas_call(kernel, out_shape=(jax.ShapeDtypeStruct((1, GROUP), F32),...  119 us
    unnamed x3, local copies, waits for them, and re-layouts  4.4 us

profile of v1, /device:TPU:1, one launch (start us, length us, event | category | flops | bytes accessed | tf_op | source)
XLA Modules:
  0.0 124.9 jit_solution(9245773389196672549)
XLA Ops:
  0.6 1.3 %pad_add_fusion.meta = s32[3,512]{1,0:T(4,128)} fusion(s32[1,512]{1,0:T(1,128)} %bitcast.8, s32[1,512]{1,0:T(1,128)} %bitcast.9, s32[1,512]{1,0:T(1,128)} %bitcast.10), kind=kLoop, calls=%fused_computation | loop fusion | flops 3072 | bytes 12288 | tf_op jit(solution)/shard_map/stack | solution.py:509
  2.0 118.5 %shard_map.94 = (f32[1,512]{1,0:T(1,128)}, f32[128,128]{1,0:T(8,128)}, f32[512,128]{1,0:T(8,128)}) custom-call(s32[3,512]{1,0:T(4,128)} %pad_add_fusion.meta, bf16[1000,128]{1,0:T(8,128)(2,1)} %bitcast.7, bf16[128,128]{1,0:T(8,128)(2,1)} %ent_s.1, bf16[1000,4131]{1,0:T(8,128)(2,1)} %bitcast.6, bf16[4131,128]{1,0:T(8,128)(2,1)} %rel_s.1), custom_call_target="tpu_custom_call" | custom-call | tf_op jit(solution)/shard_map/pallas_call | solution.py:513
  120.5 1.3 %copy.13 = f32[512]{0:T(512)} copy(f32[512]{0:T(512)} %bitcast.11) | data formatting | bytes 4096
  121.8 1.5 %copy.14 = f32[128,128]{1,0:T(8,128)} copy(f32[128,128]{1,0:T(8,128)} %get-tuple-element.13) | data formatting | bytes 131072
  123.2 1.7 %copy.15 = f32[512,128]{1,0:T(8,128)} copy(f32[512,128]{1,0:T(8,128)} %get-tuple-element.14) | data formatting | bytes 524288

commit v2 on v1

--- a/solution.py
+++ b/solution.py
@@ -34,7 +34,9 @@
 
 
 def kernel(
-    meta,
+    anchors,
+    relation_ids,
+    flags,
     ent_t,
     ent_s,
     rel_t,
@@ -71,6 +73,7 @@
     ftb,
     fsb,
     qst,
+    gbuf,
     eg_own,
     eg_s,
     eg_sr,
@@ -83,6 +86,9 @@
     qgz,
     qgr,
     qgo,
+    idv,
+    ent_v,
+    ens_v,
     loc_sem,
     send_sem,
     recv_sem,
@@ -105,10 +111,10 @@
 
     mate = (q, zl * 2 + 1 - core)
 
-    rt_copy = pltpu.make_async_copy(rel_t, rtv, loc_sem.at[0])
-    rt_copy.start()
-    rs_copy = pltpu.make_async_copy(rel_s, rsv, loc_sem.at[1])
-    rs_copy.start()
+    moves = ((ent_t, ent_v), (ent_s, ens_v), (anchors, idv.at[0]), (relation_ids, idv.at[1]), (flags, idv.at[2]))
+    moves = [pltpu.make_async_copy(a, b, loc_sem.at[2 + i]) for i, (a, b) in enumerate(moves)]
+    for move in moves:
+        move.start()
 
     barrier = pltpu.get_barrier_semaphore()
     peers = [(dev(d, 0), e) for d in (1, 2, 3)]
@@ -118,14 +124,22 @@
     for peer in peers:
         pl.semaphore_signal(barrier, inc=1, device_id=peer, device_id_type=MESH)
 
-    slab[0, 0:ENT, :] = ent_s[...]
-    wide[0 : 2 * HALF, :] = ent_t[...].astype(F32)
+    rt_copy = pltpu.make_async_copy(rel_t, rtv, loc_sem.at[0])
+    rs_copy = pltpu.make_async_copy(rel_s, rsv, loc_sem.at[1])
+    for move in moves:
+        move.wait()
+
+    slab[0, 0:ENT, :] = ens_v[...]
+    wide[0 : 2 * HALF, :] = ent_v[...].astype(F32)
     wide[2 * HALF : 2 * PAD, :] = jnp.zeros((2 * PAD - 2 * HALF, ENT), F32)
     row = lax.broadcasted_iota(jnp.int32, (PAD, ENT), 0)
     slab[0, ENT : ENT + PAD, :] = jnp.where(row < HALF, wide[0:PAD, :], 0.0).astype(BF)
     slab[0, ENT + PAD : BLK, :] = pltpu.roll(wide[...], 2 * PAD - HALF, 0)[0:PAD].astype(BF)
     mids[zh] = jnp.zeros((8, GROUP), jnp.int32)
-    mids[zh, 0:3, :] = meta[...]
+    for i in range(3):
+        mids[zh, i : i + 1, :] = idv[i]
+    rt_copy.start()
+    rs_copy.start()
     pl.semaphore_wait(barrier, len(peers))
 
     sent = []
@@ -156,50 +170,61 @@
             device_id_type=MESH,
         ).wait_recv()
 
-    def block(k, half=None):
-        if half is None:
-            return slab.at[k]
+    def block(k, half):
         return slab.at[k, pl.ds(half * CUT, CUT), :]
 
-    def push(src, dst, target, half=None):
+    def push(src, dst, target, half):
         ship(("slab", dst, half), block(src, half), block(dst, half), (target, e))
 
-    def got(k, half=None):
+    def got(k, half):
         await_at(("slab", k, half), block(k, half))
 
     def f_start():
-        push(slot(0, 0), slot(0, 3), dev(1, 0))
-        push(slot(0, 0), slot(0, 1), dev(3, 0))
-
-    def s_start(fd):
-        push(slot(0, fd), slot(3, fd), dev(0, 1))
-        push(slot(0, fd), slot(1, fd), dev(0, 3))
-
-    def f_step(fd):
-        got(slot(0, fd))
-        push(slot(0, fd), slot(0, 2), dev(1 if fd == 3 else 3, 0), 0 if fd == 3 else 1)
-        s_start(fd)
+        for up, down in ((0, 1), (1, 0)):
+            push(slot(0, 0), slot(0, 3), dev(1, 0), up)
+            push(slot(0, 0), slot(0, 1), dev(3, 0), down)
+
+    def s_start(fd, half):
+        for sd in (1, 3) if half == 0 else (3, 1):
+            push(slot(0, fd), slot(4 - sd, fd), dev(0, sd), half)
+
+    def f_turn():
+        got(slot(0, 3), 0)
+        push(slot(0, 3), slot(0, 2), dev(1, 0), 0)
+        got(slot(0, 1), 1)
+        push(slot(0, 1), slot(0, 2), dev(3, 0), 1)
+        s_start(3, 0)
+        s_start(1, 1)
+        got(slot(0, 3), 1)
+        s_start(3, 1)
+        got(slot(0, 1), 0)
+        s_start(1, 0)
 
     def f_last():
-        got(slot(0, 2), 0)
-        got(slot(0, 2), 1)
-        s_start(2)
-
-    def s_step(fd):
-        got(slot(3, fd))
+        for half in range(2):
+            got(slot(0, 2), half)
+            s_start(2, half)
+
+    def s_turn(fd):
+        got(slot(3, fd), 0)
         push(slot(3, fd), slot(2, fd), dev(0, 1), 0)
-        got(slot(1, fd))
+        got(slot(1, fd), 1)
         push(slot(1, fd), slot(2, fd), dev(0, 3), 1)
+
+    def s_rest():
+        for fd in (0, 3, 1, 2):
+            got(slot(3, fd), 1)
+            got(slot(1, fd), 0)
 
     lane = lax.broadcasted_iota(jnp.int32, (ROWS, ENT), 1)
 
     def one_hot(ids, at):
         return jnp.where(ids - at == lane[: ids.shape[0]], 1.0, 0.0).astype(BF)
 
-    def pick(sd, new=False):
-        ks = [slot(sd, fd) for fd in range(4)]
+    def pick(sd, new=False, fds=(0, 1, 2, 3)):
+        ks = [slot(sd, fd) for fd in fds]
         hot = jnp.concatenate(
-            [one_hot(idb[...], e * 4096 + dev(fd, sd) * ENT) for fd in range(4)], axis=1
+            [one_hot(idb[...], e * 4096 + dev(fd, sd) * ENT) for fd in fds], axis=1
         )
         value = dot_nn(hot, jnp.concatenate([slab[k, 0:ENT, :] for k in ks], axis=0))
         tbuf[4, :, 0:ENT] = value if new else tbuf[4, :, 0:ENT] + value
@@ -227,10 +252,11 @@
             rsacc[...] += dot_nn(hots, rsv[pl.ds(at, 512), :])
 
     f_start()
-    s_start(0)
+    s_start(0, 0)
+    s_start(0, 1)
     ship("ids", mids.at[zh], mids.at[zh], zdev(4))
-    f_step(3)
-    f_step(1)
+    f_turn()
+    s_turn(0)
     await_at("ids", mids.at[1 - zh])
     mrow[...] = jnp.zeros_like(mrow)
     for g in range(2):
@@ -240,29 +266,42 @@
         wanted = jnp.broadcast_to(flat[:, 0:1], (GROUP, ENT)).astype(jnp.int32)
         idb[g * GROUP : (g + 1) * GROUP, :] = wanted
     f_last()
-    s_step(0)
+    s_turn(3)
+    s_turn(1)
     rt_copy.wait()
     rs_copy.wait()
+    pick(0, True)
+    s_turn(2)
     relations()
-    s_step(3)
-    s_step(1)
-    pick(0, True)
-    s_step(2)
+    s_rest()
     pick(3)
     pick(1)
-    for fd in range(4):
-        got(slot(2, fd), 0)
-        got(slot(2, fd), 1)
-    pick(2)
-
-    abuf[:, 0:ENT] = tbuf[4, :, 0:ENT].astype(BF)
-    for h in range(4):
-        abuf[:, ENT + h * 256 : ENT + (h + 1) * 256] = tbuf[h].astype(BF)
-    other = pl.multiple_of((1 - core) * GROUP, GROUP)
-    ship("pair", abuf.at[pl.ds(other, GROUP), :], dbuf, mate)
-    await_at("pair", dbuf)
-    kept = pl.multiple_of(core * GROUP, GROUP)
-    sumb[...] = (abuf[pl.ds(kept, GROUP), :].astype(F32) + dbuf[...].astype(F32)).astype(BF)
+    for fds in ((0, 3), (1, 2)):
+        for fd in fds:
+            got(slot(2, fd), 0)
+            got(slot(2, fd), 1)
+        pick(2, fds=fds)
+
+    def shard(d, c=None):
+        at = lax.rem(z + d, 8) * SHARD
+        return pl.ds(pl.multiple_of(at if c is None else c * GROUP + at, SHARD), SHARD)
+
+    order = (4, 3, 5, 2, 6, 1, 7, 0)
+    for d in order:
+        theirs = shard(d, 1 - core)
+        abuf[shard(d), 0:ENT] = tbuf[4, theirs, 0:ENT].astype(BF)
+        for h in range(4):
+            abuf[shard(d), ENT + h * 256 : ENT + (h + 1) * 256] = tbuf[h, theirs, :].astype(BF)
+        ship(("pair", d), abuf.at[shard(d), :], dbuf.at[shard(d), :], mate)
+
+    def merge_cores(d):
+        await_at(("pair", d), dbuf.at[shard(d), :])
+        came = dbuf[shard(d), :].astype(F32)
+        ours = shard(d, core)
+        sumb[shard(d), 0:ENT] = (tbuf[4, ours, 0:ENT] + came[:, 0:ENT]).astype(BF)
+        for h in range(4):
+            cols = slice(ENT + h * 256, ENT + (h + 1) * 256)
+            sumb[shard(d), cols] = (tbuf[h, ours, :] + came[:, cols]).astype(BF)
 
     def part(d, half):
         return pl.ds(pl.multiple_of(lax.rem(z + d, 8) * SHARD + half * BIT, BIT), BIT)
@@ -281,10 +320,14 @@
         await_at(("ring", way, role, j), rbuf.at[at])
         return rbuf[at].astype(F32)
 
+    merge_cores(4)
     for way in range(2):
         ring_send(way, 0, 4)
     for way in range(2):
+        merge_cores(3 if way == 0 else 5)
         ring_send(way, 1, 3)
+    for d in order[3:]:
+        merge_cores(d)
     for role, j in ((0, 4), (1, 3), (0, 3), (1, 2), (0, 2)):
         for way in range(2):
             came = ring_wait(way, role, j)
@@ -326,58 +369,79 @@
             ring_pass(way, role, 1)
     for h in range(2):
         ship(("mate", 0, h), bit(0, h), bit(0, h), mate)
-    came = [(0, h) for h in range(2)]
-    for role, j in ((0, 1), (1, 1), (0, 2), (1, 2), (0, 3), (1, 3), (0, 4)):
+
+    def pass_on(role, j):
         for way in range(2):
             h = chain(way, role)
             d = 8 - j if way == 0 else j
             await_at(("pass", way, role, j), bit(d, h))
-            if j < 4 - role:
+            if j < 3:
                 ring_pass(way, role, j + 1)
+            if (role, j) == (0, 2):
+                ship(("pass", way, 0, 4), bit(d, h), bit(d, h), zdev(2 if way == 0 else 6))
             ship(("mate", d, h), bit(d, h), bit(d, h), mate)
-            came.append((d, h))
-    for d, h in came:
-        await_at(("mate", d, h), bit(d, h, True))
-
-    mxt[...] = jnp.full_like(mxt, -jnp.inf)
-    mxs[...] = jnp.full_like(mxs, -jnp.inf)
-
-    @pl.loop(0, 8)
-    def _(p):
-        k = 2 * p
-        right = jnp.concatenate([slab[k, ENT:BLK, :], slab[k + 1, ENT:BLK, :]], axis=1)
-        t = dot_nn(qbuf[:, ENT:BLK], right)
-        right = jnp.concatenate([slab[k, 0:ENT, :], slab[k + 1, 0:ENT, :]], axis=0)
-        s = dot_nt(qbuf[:, 0:ENT], right)
-        tbuf[p] = t
-        sbuf[p] = s
-        mxt[...] = jnp.maximum(mxt[...], jnp.maximum(t[:, 0:ENT], t[:, ENT:]))
-        mxs[...] = jnp.maximum(mxs[...], jnp.maximum(s[:, 0:ENT], s[:, ENT:]))
-
-    mxt[...] = jnp.broadcast_to(jnp.max(mxt[...], axis=1, keepdims=True), (ROWS, ENT))
-    mxs[...] = jnp.broadcast_to(jnp.max(mxs[...], axis=1, keepdims=True), (ROWS, ENT))
-
-    @pl.loop(0, ROWS // 64)
-    def _(r):
-        rows = pl.ds(pl.multiple_of(r * 64, 64), 64)
-        top_t, top_s = mxt[rows, :], mxs[rows, :]
-
-        def step(p, carry):
-            zt, w, zs = carry
+
+    def score(start, stride, number):
+        ds = [(start + stride * i) % 8 for i in range(number)]
+        for d in ds:
             for h in range(2):
-                cols = slice(h * ENT, (h + 1) * ENT)
-                t, s = tbuf[p, rows, cols], sbuf[p, rows, cols]
-                et, es = jnp.exp(t - top_t), jnp.exp(s - top_s)
-                zt, w, zs = zt + et, w + et * (t - s), zs + es
-                tbuf[p, rows, cols] = et
-                sbuf[p, rows, cols] = es
-            return zt, w, zs
-
-        zero = jnp.zeros((64, ENT), F32)
-        zt, w, zs = lax.fori_loop(0, 8, step, (zero, zero, zero))
-        zt_acc[rows, :] = zt
-        w_acc[rows, :] = w
-        zs_acc[rows, :] = zs
+                await_at(("mate", d, h), bit(d, h, True))
+
+        def rows_at(g, d):
+            return pl.ds(pl.multiple_of(g * GROUP + lax.rem(z + d, 8) * SHARD, SHARD), SHARD)
+
+        pieces = [rows_at(g, d) for g in range(2) for d in ds]
+        for rows in pieces:
+            mxt[rows, :] = jnp.full((SHARD, ENT), -jnp.inf)
+            mxs[rows, :] = jnp.full((SHARD, ENT), -jnp.inf)
+
+        @pl.loop(0, 8)
+        def _(p):
+            k = 2 * p
+            left = jnp.concatenate([qbuf[rows, :] for rows in pieces], axis=0)
+            right = jnp.concatenate([slab[k, ENT:BLK, :], slab[k + 1, ENT:BLK, :]], axis=1)
+            t = dot_nn(left[:, ENT:BLK], right)
+            right = jnp.concatenate([slab[k, 0:ENT, :], slab[k + 1, 0:ENT, :]], axis=0)
+            s = dot_nt(left[:, 0:ENT], right)
+            for i, rows in enumerate(pieces):
+                ti, si = t[i * SHARD : (i + 1) * SHARD], s[i * SHARD : (i + 1) * SHARD]
+                tbuf[p, rows, :] = ti
+                sbuf[p, rows, :] = si
+                mxt[rows, :] = jnp.maximum(mxt[rows, :], jnp.maximum(ti[:, 0:ENT], ti[:, ENT:]))
+                mxs[rows, :] = jnp.maximum(mxs[rows, :], jnp.maximum(si[:, 0:ENT], si[:, ENT:]))
+
+        @pl.loop(0, 2 * number)
+        def _(r):
+            g = lax.div(r, number)
+            rows = rows_at(g, start + stride * (r - g * number))
+            top_t = jnp.broadcast_to(jnp.max(mxt[rows, :], axis=1, keepdims=True), (SHARD, ENT))
+            top_s = jnp.broadcast_to(jnp.max(mxs[rows, :], axis=1, keepdims=True), (SHARD, ENT))
+            mxt[rows, :] = top_t
+            mxs[rows, :] = top_s
+
+            def step(p, carry):
+                zt, w, zs = carry
+                for h in range(2):
+                    cols = slice(h * ENT, (h + 1) * ENT)
+                    t, s = tbuf[p, rows, cols], sbuf[p, rows, cols]
+                    et, es = jnp.exp(t - top_t), jnp.exp(s - top_s)
+                    zt, w, zs = zt + et, w + et * (t - s), zs + es
+                    tbuf[p, rows, cols] = et
+                    sbuf[p, rows, cols] = es
+                return zt, w, zs
+
+            zero = jnp.zeros((SHARD, ENT), F32)
+            zt, w, zs = lax.fori_loop(0, 8, step, (zero, zero, zero))
+            zt_acc[rows, :] = zt
+            w_acc[rows, :] = w
+            zs_acc[rows, :] = zs
+
+    for role, j in ((0, 1), (1, 1), (0, 2), (1, 2)):
+        pass_on(role, j)
+    score(6, 1, 5)
+    for role, j in ((0, 3), (1, 3), (0, 4)):
+        pass_on(role, j)
+    score(3, 1, 3)
 
     table = jnp.where(lane == 0, mxt[...], 0.0)
     table = jnp.where(lane == 1, jnp.sum(zt_acc[...], axis=1, keepdims=True), table)
@@ -427,32 +491,48 @@
         fsb[g * GROUP : (g + 1) * GROUP, :] = jnp.broadcast_to(flipped[:, 1:2], (GROUP, ENT))
 
     qg[...] = jnp.zeros_like(qg)
-    for sd in (2, 1, 3, 0):
-
+
+    @pl.loop(0, 8)
+    def _(p):
+        halves = []
+        for h in range(2):
+            cols = slice(h * ENT, (h + 1) * ENT)
+            g = sbuf[p, :, cols] * fsb[...] - tbuf[p, :, cols] * ftb[...]
+            halves.append(g.astype(BF))
+        g = jnp.concatenate(halves, axis=1)
+        gbuf[p] = g
+        right = jnp.concatenate([slab[2 * p, 0:ENT, :], slab[2 * p + 1, 0:ENT, :]], axis=0)
+        qg[...] += dot_nn(g, right)
+
+    other = pl.multiple_of((1 - core) * GROUP, GROUP)
+    kept = pl.multiple_of(core * GROUP, GROUP)
+    qgb[...] = qg[pl.ds(other, GROUP), :].astype(BF)
+    ship("pair grad", qgb, qgd, mate)
+
+    def entities(sd):
         @pl.loop(0, 2)
-        def _(i, sd=sd):
-            p = sd * 2 + i
-            halves = []
-            for h in range(2):
-                cols = slice(h * ENT, (h + 1) * ENT)
-                g = sbuf[p, :, cols] * fsb[...] - tbuf[p, :, cols] * ftb[...]
-                halves.append(g.astype(BF))
-            g = jnp.concatenate(halves, axis=1)
-            grad = dot_nn(qst[...], g)
+        def _(i):
+            grad = dot_nn(qst[...], gbuf[sd * 2 + i])
             for h in range(2):
                 cols = slice(h * ENT, (h + 1) * ENT)
                 if sd:
                     eg_s[sd - 1, 2 * i + h] = grad[:, cols].astype(BF)
                 else:
                     eg_own[2 * i + h] = grad[:, cols]
-            right = jnp.concatenate([slab[2 * p, 0:ENT, :], slab[2 * p + 1, 0:ENT, :]], axis=0)
-            qg[...] += dot_nn(g, right)
 
         if sd:
             ship(("second", sd), eg_s.at[sd - 1], eg_sr.at[sd - 1], (dev(0, sd), e))
 
-    qgb[...] = qg[pl.ds(other, GROUP), :].astype(BF)
-    ship("pair grad", qgb, qgd, mate)
+    entities(2)
+    entities(1)
+    await_at("pair grad", qgd)
+    qgsum[...] = qg[pl.ds(kept, GROUP), :] + qgd[...].astype(F32)
+    qgz[...] = qgsum[...].astype(BF)
+    for d in range(1, 8):
+        at = pl.multiple_of(lax.rem(z + d, 8) * SHARD, SHARD)
+        ship(("shard", d), qgz.at[pl.ds(at, SHARD), :], qgr.at[d - 1], zdev(d))
+    entities(3)
+    entities(0)
     for sd in (1, 3, 2):
         await_at(("second", sd), eg_sr.at[sd - 1])
     for fd in (2, 1, 3, 0):
@@ -464,29 +544,23 @@
             ship(("first", fd), eg_f.at[fd - 1], eg_fr.at[fd - 1], (dev(fd, 0), e))
         else:
             near = v
-    await_at("pair grad", qgd)
-    qgsum[...] = qg[pl.ds(kept, GROUP), :] + qgd[...].astype(F32)
-    qgz[...] = qgsum[...].astype(BF)
+    total = qgsum[pl.ds(pl.multiple_of(z * SHARD, SHARD), SHARD), :]
     for d in range(1, 8):
-        at = pl.multiple_of(lax.rem(z + d, 8) * SHARD, SHARD)
-        ship(("shard", d), qgz.at[pl.ds(at, SHARD), :], qgr.at[d - 1], zdev(d))
+        await_at(("shard", d), qgr.at[d - 1])
+    for d in range(1, 8):
+        total = total + qgr[d - 1].astype(F32)
+
+    def out_rows(d):
+        return qgo.at[core, pl.ds(pl.multiple_of(lax.rem(z + d, 8) * SHARD, SHARD), SHARD), :]
+
+    qgo[core, pl.ds(pl.multiple_of(z * SHARD, SHARD), SHARD), :] = total.astype(BF)
+    for d in range(1, 8):
+        ship(("sum", d), out_rows(0), out_rows(0), zdev(d))
     for fd in (1, 3, 2):
         await_at(("first", fd), eg_fr.at[fd - 1])
     for fd in (1, 2, 3):
         near = near + eg_fr[fd - 1].astype(F32)
     eg_out[...] = jnp.transpose(near)
-    total = qgsum[pl.ds(pl.multiple_of(z * SHARD, SHARD), SHARD), :]
-    for d in range(1, 8):
-        await_at(("shard", d), qgr.at[d - 1])
-    for d in range(1, 8):
-        total = total + qgr[d - 1].astype(F32)
-
-    def out_rows(d):
-        return qgo.at[core, pl.ds(pl.multiple_of(lax.rem(z + d, 8) * SHARD, SHARD), SHARD), :]
-
-    qgo[core, pl.ds(pl.multiple_of(z * SHARD, SHARD), SHARD), :] = total.astype(BF)
-    for d in range(1, 8):
-        ship(("sum", d), out_rows(0), out_rows(0), zdev(d))
     for d in range(1, 8):
         await_at(("sum", d), out_rows(8 - d))
     ship("pair sum", qgo.at[core], qgo.at[core], mate)
@@ -495,6 +569,12 @@
 
     for copy in sent:
         copy.wait_send()
+
+
+def finish(div, eg, qg, div_out, eg_out, qg_out):
+    div_out[...] = div[...]
+    eg_out[...] = eg[...]
+    qg_out[...] = qg[...]
 
 
 def per_device(
@@ -506,7 +586,7 @@
     teacher_relations,
     student_relations,
 ):
-    meta = jnp.stack([anchor_ids, relation_ids, side_flags], axis=0)
+    rows = [v.reshape(1, GROUP) for v in (anchor_ids, relation_ids, side_flags)]
     vmem = pl.BlockSpec(memory_space=pltpu.VMEM)
     hbm = pl.BlockSpec(memory_space=pl.ANY)
     big = (ROWS, ENT)
@@ -517,7 +597,7 @@
             jax.ShapeDtypeStruct((ENT, ENT), F32),
             jax.ShapeDtypeStruct((GROUP, ENT), F32),
         ),
-        in_specs=[vmem, vmem, vmem, hbm, hbm],
+        in_specs=[hbm] * 7,
         out_specs=(vmem, vmem, vmem),
         scratch_shapes=[
             pltpu.VMEM((16, BLK, ENT), BF),
@@ -528,7 +608,7 @@
             pltpu.VMEM((ENT, GROUP), F32),
             pltpu.VMEM(big, F32),
             pltpu.VMEM(big, jnp.int32),
-            pltpu.VMEM((ROWS, BLK), BF),
+            pltpu.VMEM((GROUP, BLK), BF),
             pltpu.VMEM((GROUP, BLK), BF),
             pltpu.VMEM((GROUP, BLK), BF),
             pltpu.VMEM((14, BIT, BLK), BF),
@@ -549,6 +629,7 @@
             pltpu.VMEM(big, F32),
             pltpu.VMEM(big, F32),
             pltpu.VMEM((ENT, ROWS), BF),
+            pltpu.VMEM((8, ROWS, 256), BF),
             pltpu.VMEM((4, ENT, ENT), F32),
             pltpu.VMEM((3, 4, ENT, ENT), BF),
             pltpu.VMEM((3, 4, ENT, ENT), BF),
@@ -561,14 +642,27 @@
             pltpu.VMEM((GROUP, ENT), BF),
             pltpu.VMEM((7, SHARD, ENT), BF),
             pltpu.VMEM((2, GROUP, ENT), BF),
-            pltpu.SemaphoreType.DMA((2,)),
-            pltpu.SemaphoreType.DMA((110,)),
-            pltpu.SemaphoreType.DMA((110,)),
+            pltpu.VMEM((3, 1, GROUP), jnp.int32),
+            pltpu.VMEM((2 * HALF, ENT), BF),
+            pltpu.VMEM((ENT, ENT), BF),
+            pltpu.SemaphoreType.DMA((7,)),
+            pltpu.SemaphoreType.DMA((120,)),
+            pltpu.SemaphoreType.DMA((120,)),
         ],
         compiler_params=pltpu.CompilerParams(
             collective_id=0, has_side_effects=True, vmem_limit_bytes=60 * 2**20
         ),
-    )(meta, teacher_entities.T, student_entities, teacher_relations.T, student_relations)
+    )(*rows, teacher_entities.T, student_entities, teacher_relations.T, student_relations)
+    div, eg, qg = pl.pallas_call(
+        finish,
+        out_shape=(
+            jax.ShapeDtypeStruct((1, GROUP), F32),
+            jax.ShapeDtypeStruct((ENT, ENT), F32),
+            jax.ShapeDtypeStruct((GROUP, ENT), F32),
+        ),
+        in_specs=[vmem, vmem, vmem],
+        out_specs=(vmem, vmem, vmem),
+    )(div, eg, qg)
     return div.reshape(GROUP), eg, qg
 
 

time: 125 us -> 117 us (0.936)
  local copies, waits for them, and re-layouts: 4.4 us -> 0 us
  Pallas kernels: 119 us -> 116 us
  other arithmetic: 1.32 us -> 0 us
    unnamed x3 -> x0, local copies, waits for them, and re-layouts: 4.4 us -> none
    pallas_call x1, Pallas kernels: 119 us -> 114 us  [per_device(): pl.pallas_call(kernel, out_shape=(jax.ShapeDtypeStruct((1, GROUP), F32),...]
    pallas_call x0 -> x1, Pallas kernels: none -> 1.73 us  [per_device(): pl.pallas_call(finish, out_shape=(jax.ShapeDtypeStruct((1, GROUP), F32),...]
    another operation x1 -> x0, other arithmetic: 1.32 us -> none  [per_device(): meta = jnp.stack([anchor_ids, relation_ids, side_flags], axis=0)]
where the time goes in v2:
time: 117 us
  Pallas kernels  116 us (99%)
    pallas_call x1, Pallas kernels, per_device(): pl.pallas_call(kernel, out_shape=(jax.ShapeDtypeStruct((1, GROUP), F32),...  114 us

profile of v2, /device:TPU:1, one launch (start us, length us, event | category | flops | bytes accessed | tf_op | source)
XLA Modules:
  0.0 116.7 jit_solution(4468447520913671696)
XLA Ops:
  0.6 114.3 %shard_map.94 = (f32[1,512]{1,0:T(1,128)}, f32[128,128]{1,0:T(8,128)}, f32[512,128]{1,0:T(8,128)}) custom-call(s32[1,512]{1,0:T(1,128)} %bitcast.8, s32[1,512]{1,0:T(1,128)} %bitcast.9, s32[1,512]{1,0:T(1,128)} %bitcast.10, bf16[1000,128]{1,0:T(8,128)(2,1)} %bitcast.7, bf16[128,128]{1,0:T(8,128)(2,1)} %ent_s.1, bf16[1000,4131]{1,0:T(8,128)(2,1)} %bitcast.6, ...), custom_call_target="tpu_custom_call" | custom-call | tf_op jit(solution)/shard_map/pallas_call | solution.py:593
  115.0 1.7 %shard_map.95 = (f32[1,512]{1,0:T(1,128)}, f32[128,128]{1,0:T(8,128)}, f32[512,128]{1,0:T(8,128)}) custom-call(f32[1,512]{1,0:T(1,128)} %get-tuple-element.9.div, f32[128,128]{1,0:T(8,128)} %get-tuple-element.10.eg, f32[512,128]{1,0:T(8,128)} %get-tuple-element.11.qg), custom_call_target="tpu_custom_call" | custom-call | tf_op jit(solution)/shard_map/pallas_call | solution.py:656

commit v3 on v2

--- a/solution.py
+++ b/solution.py
@@ -323,11 +323,10 @@
     merge_cores(4)
     for way in range(2):
         ring_send(way, 0, 4)
+    for d in order[1:]:
+        merge_cores(d)
     for way in range(2):
-        merge_cores(3 if way == 0 else 5)
         ring_send(way, 1, 3)
-    for d in order[3:]:
-        merge_cores(d)
     for role, j in ((0, 4), (1, 3), (0, 3), (1, 2), (0, 2)):
         for way in range(2):
             came = ring_wait(way, role, j)
@@ -431,14 +430,18 @@
                 return zt, w, zs
 
             zero = jnp.zeros((SHARD, ENT), F32)
-            zt, w, zs = lax.fori_loop(0, 8, step, (zero, zero, zero))
+            zt, w, zs = lax.fori_loop(0, 8, step, (zero, zero, zero), unroll=True)
             zt_acc[rows, :] = zt
             w_acc[rows, :] = w
             zs_acc[rows, :] = zs
 
-    for role, j in ((0, 1), (1, 1), (0, 2), (1, 2)):
-        pass_on(role, j)
-    score(6, 1, 5)
+    score(0, 1, 1)
+    pass_on(0, 1)
+    pass_on(1, 1)
+    score(1, 6, 2)
+    pass_on(0, 2)
+    pass_on(1, 2)
+    score(2, 4, 2)
     for role, j in ((0, 3), (1, 3), (0, 4)):
         pass_on(role, j)
     score(3, 1, 3)

time: 117 us -> 113 us (0.966)
  Pallas kernels: 116 us -> 112 us
    pallas_call x1, Pallas kernels: 114 us -> 110 us  [per_device(): pl.pallas_call(kernel, out_shape=(jax.ShapeDtypeStruct((1, GROUP), F32),...]
where the time goes in v3:
time: 113 us; the launch traced here: 112 us
  Pallas kernels  112 us (99%)
    pallas_call x1, Pallas kernels, per_device(): pl.pallas_call(kernel, out_shape=(jax.ShapeDtypeStruct((1, GROUP), F32),...  110 us

profile of v3, /device:TPU:1, one launch (start us, length us, event | category | flops | bytes accessed | tf_op | source)
XLA Modules:
  0.0 112.3 jit_solution(8208672587778663394)
XLA Ops:
  0.6 109.9 %shard_map.94 = (f32[1,512]{1,0:T(1,128)}, f32[128,128]{1,0:T(8,128)}, f32[512,128]{1,0:T(8,128)}) custom-call(s32[1,512]{1,0:T(1,128)} %bitcast.8, s32[1,512]{1,0:T(1,128)} %bitcast.9, s32[1,512]{1,0:T(1,128)} %bitcast.10, bf16[1000,128]{1,0:T(8,128)(2,1)} %bitcast.7, bf16[128,128]{1,0:T(8,128)(2,1)} %ent_s.1, bf16[1000,4131]{1,0:T(8,128)(2,1)} %bitcast.6, ...), custom_call_target="tpu_custom_call" | custom-call | tf_op jit(solution)/shard_map/pallas_call | solution.py:596
  110.5 1.7 %shard_map.95 = (f32[1,512]{1,0:T(1,128)}, f32[128,128]{1,0:T(8,128)}, f32[512,128]{1,0:T(8,128)}) custom-call(f32[1,512]{1,0:T(1,128)} %get-tuple-element.9.div, f32[128,128]{1,0:T(8,128)} %get-tuple-element.10.eg, f32[512,128]{1,0:T(8,128)} %get-tuple-element.11.qg), custom_call_target="tpu_custom_call" | custom-call | tf_op jit(solution)/shard_map/pallas_call | solution.py:659

commit v4 on v3

--- a/solution.py
+++ b/solution.py
@@ -473,7 +473,7 @@
     st[z] = jnp.zeros((8, GROUP), F32)
     for i, v in enumerate(merge([own_st[core], mate_st[...]])):
         st[z, i : i + 1, :] = v
-    for d in range(1, 8):
+    for d in order[:7]:
         ship(("stats", d), st.at[z], st.at[z], zdev(d))
     for d in range(1, 8):
         await_at(("stats", d), st.at[lax.rem(z + 8 - d, 8)])
@@ -495,22 +495,32 @@
 
     qg[...] = jnp.zeros_like(qg)
 
-    @pl.loop(0, 8)
-    def _(p):
-        halves = []
-        for h in range(2):
-            cols = slice(h * ENT, (h + 1) * ENT)
-            g = sbuf[p, :, cols] * fsb[...] - tbuf[p, :, cols] * ftb[...]
-            halves.append(g.astype(BF))
-        g = jnp.concatenate(halves, axis=1)
-        gbuf[p] = g
-        right = jnp.concatenate([slab[2 * p, 0:ENT, :], slab[2 * p + 1, 0:ENT, :]], axis=0)
-        qg[...] += dot_nn(g, right)
-
     other = pl.multiple_of((1 - core) * GROUP, GROUP)
     kept = pl.multiple_of(core * GROUP, GROUP)
+
+    def weights(rows):
+        @pl.loop(0, 8)
+        def _(p):
+            halves = []
+            for h in range(2):
+                cols = slice(h * ENT, (h + 1) * ENT)
+                g = sbuf[p, rows, cols] * fsb[rows, :] - tbuf[p, rows, cols] * ftb[rows, :]
+                halves.append(g.astype(BF))
+            g = jnp.concatenate(halves, axis=1)
+            gbuf[p, rows, :] = g
+            right = jnp.concatenate([slab[2 * p, 0:ENT, :], slab[2 * p + 1, 0:ENT, :]], axis=0)
+            qg[rows, :] += dot_nn(g, right)
+
+    weights(pl.ds(other, GROUP))
     qgb[...] = qg[pl.ds(other, GROUP), :].astype(BF)
     ship("pair grad", qgb, qgd, mate)
+    weights(pl.ds(kept, GROUP))
+    await_at("pair grad", qgd)
+    qgsum[...] = qg[pl.ds(kept, GROUP), :] + qgd[...].astype(F32)
+    qgz[...] = qgsum[...].astype(BF)
+    for d in order[:7]:
+        at = pl.multiple_of(lax.rem(z + d, 8) * SHARD, SHARD)
+        ship(("shard", d), qgz.at[pl.ds(at, SHARD), :], qgr.at[d - 1], zdev(d))
 
     def entities(sd):
         @pl.loop(0, 2)
@@ -528,12 +538,6 @@
 
     entities(2)
     entities(1)
-    await_at("pair grad", qgd)
-    qgsum[...] = qg[pl.ds(kept, GROUP), :] + qgd[...].astype(F32)
-    qgz[...] = qgsum[...].astype(BF)
-    for d in range(1, 8):
-        at = pl.multiple_of(lax.rem(z + d, 8) * SHARD, SHARD)
-        ship(("shard", d), qgz.at[pl.ds(at, SHARD), :], qgr.at[d - 1], zdev(d))
     entities(3)
     entities(0)
     for sd in (1, 3, 2):
@@ -557,7 +561,7 @@
         return qgo.at[core, pl.ds(pl.multiple_of(lax.rem(z + d, 8) * SHARD, SHARD), SHARD), :]
 
     qgo[core, pl.ds(pl.multiple_of(z * SHARD, SHARD), SHARD), :] = total.astype(BF)
-    for d in range(1, 8):
+    for d in order[:7]:
         ship(("sum", d), out_rows(0), out_rows(0), zdev(d))
     for fd in (1, 3, 2):
         await_at(("first", fd), eg_fr.at[fd - 1])

time: 113 us -> 113 us (level)
  no operation moved by 1% of the time
where the time goes in v4:
time: 113 us; the launch traced here: 112 us
  Pallas kernels  112 us (99%)
    pallas_call x1, Pallas kernels, per_device(): pl.pallas_call(kernel, out_shape=(jax.ShapeDtypeStruct((1, GROUP), F32),...  110 us

profile of v4, /device:TPU:1, one launch (start us, length us, event | category | flops | bytes accessed | tf_op | source)
XLA Modules:
  0.0 112.5 jit_solution(16947951877389041866)
XLA Ops:
  0.6 110.1 %shard_map.94 = (f32[1,512]{1,0:T(1,128)}, f32[128,128]{1,0:T(8,128)}, f32[512,128]{1,0:T(8,128)}) custom-call(s32[1,512]{1,0:T(1,128)} %bitcast.8, s32[1,512]{1,0:T(1,128)} %bitcast.9, s32[1,512]{1,0:T(1,128)} %bitcast.10, bf16[1000,128]{1,0:T(8,128)(2,1)} %bitcast.7, bf16[128,128]{1,0:T(8,128)(2,1)} %ent_s.1, bf16[1000,4131]{1,0:T(8,128)(2,1)} %bitcast.6, ...), custom_call_target="tpu_custom_call" | custom-call | tf_op jit(solution)/shard_map/pallas_call | solution.py:600
  110.7 1.7 %shard_map.95 = (f32[1,512]{1,0:T(1,128)}, f32[128,128]{1,0:T(8,128)}, f32[512,128]{1,0:T(8,128)}) custom-call(f32[1,512]{1,0:T(1,128)} %get-tuple-element.9.div, f32[128,128]{1,0:T(8,128)} %get-tuple-element.10.eg, f32[512,128]{1,0:T(8,128)} %get-tuple-element.11.qg), custom_call_target="tpu_custom_call" | custom-call | tf_op jit(solution)/shard_map/pallas_call | solution.py:663
